TPU v7x, 32 devices: a whole 2x2x4 slice. The times are simulated.
32 devices in a mesh: dp: 8 (over z, y), tensor: 4 (over x, core).
Axes of the slice: x: 2, y: 2, z: 4, core: 2. Of those that a mesh axis runs over, the one named last changes fastest.
Arguments:
- tokens: bfloat16 [8192, 1024], P(('dp', 'tensor')), may hold values from -6 to 6
- qkv_weight: bfloat16 [3, 1024, 1024], P(None, None, 'tensor'), may hold values from -0.25 to 0.25
- qv_bias: bfloat16 [2, 1024], P(None, 'tensor'), may hold values from -2 to 2
- out_weight: bfloat16 [1024, 1024], P('tensor'), may hold values from -0.5 to 0.5
- out_bias: bfloat16 [1024], replicated, may hold values from -2 to 2
- norm1_gain: bfloat16 [1024], replicated, may hold values from 0.099609375 to 1.8984375
- norm1_bias: bfloat16 [1024], replicated, may hold values from -2 to 2
- up_weight: bfloat16 [1024, 4096], P(None, 'tensor'), may hold values from -0.1875 to 0.1875
- up_bias: bfloat16 [4096], P('tensor'), may hold values from -2 to 2
- down_weight: bfloat16 [4096, 1024], P('tensor'), may hold values from -0.09375 to 0.09375
- down_bias: bfloat16 [1024], replicated, may hold values from -2 to 2
- norm2_gain: bfloat16 [1024], replicated, may hold values from 0.099609375 to 1.8984375
- norm2_bias: bfloat16 [1024], replicated, may hold values from -2 to 2
- cotangent: bfloat16 [8192, 1024], P(('dp', 'tensor')), may hold values from -7 to 7
Outputs:
- layer_out: bfloat16 [8192, 1024], P(('dp', 'tensor'))
- token_grad: float32 [8192, 1024], P(('dp', 'tensor'))
- qkv_grad: float32 [3, 1024, 1024], P(None, None, 'tensor')
- qv_bias_grad: float32 [2, 1024], P(None, 'tensor')
- out_weight_grad: float32 [1024, 1024], P('tensor')
- out_bias_grad: float32 [1024], replicated
- norm1_gain_grad: float32 [1024], replicated
- norm1_bias_grad: float32 [1024], replicated
- up_weight_grad: float32 [1024, 4096], P(None, 'tensor')
- up_bias_grad: float32 [4096], P('tensor')
- down_weight_grad: float32 [4096, 1024], P('tensor')
- down_bias_grad: float32 [1024], replicated
- norm2_gain_grad: float32 [1024], replicated
- norm2_bias_grad: float32 [1024], replicated
All inputs are finite; a program needn't handle non-finite values.
Results may differ from a plain program's by a relative error of at most 0.014.
The roundings to bfloat16 on the way count: a program that leaves them out, or rounds other values in their place, can miss the bound.
Values may be sent and summed in bfloat16 or wider, within the bound.
No kernel may reach another device: no remote copies, remote signals or barrier semaphores. Data moves between devices by JAX's collectives and lax.ppermute only.
A program may use at most 128 MiB of HBM per device.

v0:
```python
import jax
import jax.numpy as jnp
from jax import lax
from jax.sharding import PartitionSpec as P

HEAD_SIZE = 64
LENGTH = 512


EPSILON = 1e-05


def normalize(values, gain, shift):
    center = values - jnp.mean(values, -1, keepdims=True)
    spread = jnp.mean(center * center, -1, keepdims=True)
    return center * lax.rsqrt(spread + EPSILON) * gain + shift


def smooth_gate(values):
    return jax.nn.gelu(values, approximate=False)


def on_device(
    tokens,
    qkv_weight,
    qv_bias,
    out_weight,
    out_bias,
    norm1_gain,
    norm1_bias,
    up_weight,
    up_bias,
    down_weight,
    down_bias,
    norm2_gain,
    norm2_bias,
    cotangent,
):
    local_width = qkv_weight.shape[2]
    local_heads = local_width // HEAD_SIZE
    gathered = lax.all_gather(tokens, "tensor", axis=0, tiled=True)
    all_rows = gathered.shape[0]
    seq_count = all_rows // LENGTH
    block_rows = min(512, LENGTH)
    block_count = LENGTH // block_rows
    head_shape = (block_rows, local_heads, HEAD_SIZE)
    seq_shape = (LENGTH, local_heads, HEAD_SIZE)
    projected = jnp.einsum("td,kdf->ktf", gathered, qkv_weight, preferred_element_type=jnp.float32)
    bias_wide = qv_bias.astype(jnp.float32)
    query_rows = ((projected[0] + bias_wide[0]) * 0.125).astype(jnp.bfloat16)
    key_rows = projected[1].astype(jnp.bfloat16)
    value_rows = (projected[2] + bias_wide[1]).astype(jnp.bfloat16)

    def attend(position):
        seq_index = position // block_count
        row_first = seq_index * LENGTH + position % block_count * block_rows
        query_block = lax.dynamic_slice_in_dim(query_rows, row_first, block_rows, 0).reshape(
            head_shape
        )
        key_block = lax.dynamic_slice_in_dim(key_rows, seq_index * LENGTH, LENGTH, 0).reshape(
            seq_shape
        )
        value_block = lax.dynamic_slice_in_dim(value_rows, seq_index * LENGTH, LENGTH, 0).reshape(
            seq_shape
        )
        scores = jnp.einsum(
            "qhe,khe->hqk", query_block, key_block, preferred_element_type=jnp.float32
        )
        row_peak = jnp.max(scores, -1, keepdims=True)
        weights = jnp.exp(scores - row_peak)
        totals = jnp.sum(weights, -1, keepdims=True)
        attn_probs = (weights / totals).astype(jnp.bfloat16)
        head_mixed = jnp.einsum(
            "hqk,khe->qhe", attn_probs, value_block, preferred_element_type=jnp.float32
        )
        return (
            head_mixed.reshape(block_rows, local_width).astype(jnp.bfloat16),
            (row_peak + jnp.log(totals))[:, :, 0],
        )

    heads_out, log_totals = lax.map(attend, jnp.arange(seq_count * block_count, dtype=jnp.int32))
    heads_out = heads_out.reshape(all_rows, local_width)
    attn_rows = lax.psum_scatter(
        jnp.dot(heads_out, out_weight, preferred_element_type=jnp.float32),
        "tensor",
        scatter_dimension=0,
        tiled=True,
    )
    first_sum = tokens.astype(jnp.float32) + attn_rows + out_bias.astype(jnp.float32)
    normed, norm1_back = jax.vjp(
        normalize, first_sum, norm1_gain.astype(jnp.float32), norm1_bias.astype(jnp.float32)
    )
    normed_low = normed.astype(jnp.bfloat16)
    normed_all = lax.all_gather(normed_low, "tensor", axis=0, tiled=True)
    hidden_pre = jnp.dot(
        normed_all, up_weight, preferred_element_type=jnp.float32
    ) + up_bias.astype(jnp.float32)
    hidden_act, gate_back = jax.vjp(smooth_gate, hidden_pre)
    hidden_low = hidden_act.astype(jnp.bfloat16)
    feed_rows = lax.psum_scatter(
        jnp.dot(hidden_low, down_weight, preferred_element_type=jnp.float32),
        "tensor",
        scatter_dimension=0,
        tiled=True,
    )
    second_sum = normed + feed_rows + down_bias.astype(jnp.float32)
    output_full, norm2_back = jax.vjp(
        normalize, second_sum, norm2_gain.astype(jnp.float32), norm2_bias.astype(jnp.float32)
    )
    layer_out = output_full.astype(jnp.bfloat16)
    grad_second, grad_gain2, grad_shift2 = norm2_back(cotangent.astype(jnp.float32))
    grad_down_bias = jnp.sum(grad_second, 0)
    grad_second_all = lax.all_gather(grad_second.astype(jnp.bfloat16), "tensor", axis=0, tiled=True)
    grad_down = jnp.einsum(
        "tf,td->fd", hidden_low, grad_second_all, preferred_element_type=jnp.float32
    )
    grad_act = jnp.einsum(
        "td,fd->tf", grad_second_all, down_weight, preferred_element_type=jnp.float32
    )
    grad_pre = gate_back(grad_act)[0].astype(jnp.bfloat16)
    grad_up_bias = jnp.sum(grad_pre.astype(jnp.float32), 0)
    grad_up = jnp.einsum("td,tf->df", normed_all, grad_pre, preferred_element_type=jnp.float32)
    grad_normed = lax.psum_scatter(
        jnp.einsum("tf,df->td", grad_pre, up_weight, preferred_element_type=jnp.float32),
        "tensor",
        scatter_dimension=0,
        tiled=True,
    )
    grad_first, grad_gain1, grad_shift1 = norm1_back(grad_second + grad_normed)
    grad_out_bias = jnp.sum(grad_first, 0)
    small_sums = lax.psum(
        (grad_gain1, grad_shift1, grad_out_bias, grad_gain2, grad_shift2, grad_down_bias),
        ("dp", "tensor"),
    )
    grad_first_all = lax.all_gather(grad_first.astype(jnp.bfloat16), "tensor", axis=0, tiled=True)
    grad_out_weight = jnp.einsum(
        "tf,td->fd", heads_out, grad_first_all, preferred_element_type=jnp.float32
    )
    grad_heads = jnp.einsum(
        "td,fd->tf", grad_first_all, out_weight, preferred_element_type=jnp.float32
    ).astype(jnp.bfloat16)

    def attend_back(seq_index):
        base_row = seq_index * LENGTH
        key_block = lax.dynamic_slice_in_dim(key_rows, base_row, LENGTH, 0).reshape(seq_shape)
        value_block = lax.dynamic_slice_in_dim(value_rows, base_row, LENGTH, 0).reshape(seq_shape)

        def back_step(carried, block_index):
            grad_keys, grad_values = carried
            row_first = base_row + block_index * block_rows
            query_block = lax.dynamic_slice_in_dim(query_rows, row_first, block_rows, 0).reshape(
                head_shape
            )
            grad_block = lax.dynamic_slice_in_dim(grad_heads, row_first, block_rows, 0).reshape(
                head_shape
            )
            log_block = lax.dynamic_index_in_dim(
                log_totals, seq_index * block_count + block_index, 0, keepdims=False
            )
            scores = jnp.einsum(
                "qhe,khe->hqk", query_block, key_block, preferred_element_type=jnp.float32
            )
            soft_probs = jnp.exp(scores - log_block[:, :, None])
            grad_values = grad_values + jnp.einsum(
                "hqk,qhe->khe",
                soft_probs.astype(jnp.bfloat16),
                grad_block,
                preferred_element_type=jnp.float32,
            )
            grad_probs = jnp.einsum(
                "qhe,khe->hqk", grad_block, value_block, preferred_element_type=jnp.float32
            )
            grad_scores = soft_probs * (
                grad_probs - jnp.sum(soft_probs * grad_probs, -1, keepdims=True)
            )
            grad_scores = grad_scores.astype(jnp.bfloat16)
            grad_query = (
                jnp.einsum(
                    "hqk,khe->qhe", grad_scores, key_block, preferred_element_type=jnp.float32
                ).astype(jnp.bfloat16)
                * 0.125
            )
            grad_keys = grad_keys + jnp.einsum(
                "hqk,qhe->khe", grad_scores, query_block, preferred_element_type=jnp.float32
            )
            return ((grad_keys, grad_values), grad_query.reshape(block_rows, local_width))

        zero_state = jnp.zeros(seq_shape, jnp.float32)
        (grad_keys, grad_values), grad_query = lax.scan(
            back_step, (zero_state, zero_state), jnp.arange(block_count, dtype=jnp.int32)
        )
        return (
            grad_query.reshape(LENGTH, local_width),
            grad_keys.reshape(LENGTH, local_width).astype(jnp.bfloat16),
            grad_values.reshape(LENGTH, local_width).astype(jnp.bfloat16),
        )

    grad_query_all, grad_key_all, grad_value_all = lax.map(
        attend_back, jnp.arange(seq_count, dtype=jnp.int32)
    )
    grad_proj = jnp.stack(
        [
            grad_query_all.reshape(all_rows, local_width),
            grad_key_all.reshape(all_rows, local_width),
            grad_value_all.reshape(all_rows, local_width),
        ]
    )
    grad_qv_bias = jnp.stack(
        [jnp.sum(grad_proj[0].astype(jnp.float32), 0), jnp.sum(grad_proj[2].astype(jnp.float32), 0)]
    )
    grad_qkv = jnp.einsum("td,ktf->kdf", gathered, grad_proj, preferred_element_type=jnp.float32)
    grad_rows = lax.psum_scatter(
        jnp.einsum("ktf,kdf->td", grad_proj, qkv_weight, preferred_element_type=jnp.float32),
        "tensor",
        scatter_dimension=0,
        tiled=True,
    )
    token_grad = grad_first + grad_rows
    grad_qkv, grad_qv_bias, grad_out_weight, grad_up, grad_up_bias, grad_down = lax.psum(
        (grad_qkv, grad_qv_bias, grad_out_weight, grad_up, grad_up_bias, grad_down), "dp"
    )
    return (
        layer_out,
        token_grad,
        grad_qkv,
        grad_qv_bias,
        grad_out_weight,
        small_sums[2],
        small_sums[0],
        small_sums[1],
        grad_up,
        grad_up_bias,
        grad_down,
        small_sums[5],
        small_sums[3],
        small_sums[4],
    )


def solution(mesh):
    placed = (
        P(("dp", "tensor"), None),
        P(None, None, "tensor"),
        P(None, "tensor"),
        P("tensor", None),
        P(),
        P(),
        P(),
        P(None, "tensor"),
        P("tensor"),
        P("tensor", None),
        P(),
        P(),
        P(),
        P(("dp", "tensor"), None),
    )
    return jax.shard_map(
        on_device,
        mesh=mesh,
        in_specs=placed,
        out_specs=(
            P(("dp", "tensor"), None),
            P(("dp", "tensor"), None),
            P(None, None, "tensor"),
            P(None, "tensor"),
            P("tensor", None),
            P(),
            P(),
            P(),
            P(None, "tensor"),
            P("tensor"),
            P("tensor", None),
            P(),
            P(),
            P(),
        ),
        check_vma=False,
    )
```

profile of v0, /device:TPU:0, one launch (start us, length us, event | category | flops | bytes accessed | tf_op | source)
XLA Modules:
  0.0 809.2 jit_solution(15690628581118211512)
XLA Ops:
  8.0 0.8 fusion.48
  8.7 26.2 %all-gather.5.cloned.1.call-done = bf16[1024,1024]{1,0:T(8,128)(2,1)} async-done(((bf16[256,1024]{1,0:T(8,128)(2,1)}), bf16[1024,1024]{1,0:T(8,128)(2,1)}) %all-gather.5.cloned.1.call-update) | async-done | bytes 2097168 | tf_op jit(solution)/shard_map/all_gather | solution.py:41
  34.9 3.9 fusion.21
  38.9 1.0 fusion.33
  39.9 0.8 broadcast.108.clone2
  40.7 14.0 %while.37 = (s32[]{:T(128)}, bf16[2,512,256]{2,1,0:T(8,128)(2,1)}, f32[2,4,512]{2,1,0:T(4,128)S(1)}, s32[2]{0:T(128)S(1)}, bf16[1024,256]{0,1:T(8,128)(2,1)S(1)}...) while((s32[]{:T(128)}, bf16[2,512,256]{2,1,0:T(8,128)(2,1)}, ...), condition=%wide.region_3.4_spmd, body=%wide.region_0.3_spmd.sunk | while | flops 274855936 | bytes 16318655 | solution.py:81
  42.0 1.0 constant_dynamic-slice_fusion.14
  43.0 0.8 fusion.110
  44.4 1.6 fusion.112
  45.9 1.1 copy.65
  49.0 1.0 constant_dynamic-slice_fusion.14
  50.0 0.8 fusion.110
  51.4 1.6 fusion.112
  52.9 1.1 copy.65
  54.7 4.3 fusion.50
  59.8 44.0 %reduce-scatter.5.cloned.1.call-done = f32[256,1024]{1,0:T(8,128)} async-done(((f32[1024,1024]{1,0:T(8,128)}), f32[256,1024]{1,0:T(8,128)}) %reduce-scatter.5.cloned.1.call-update) | async-done | bytes 1048592 | tf_op jit(solution)/shard_map/reduce_scatter | solution.py:83
  103.8 1.6 fusion.46
  105.6 1.1 fusion.36
  106.8 22.7 %all-gather.7.cloned.1.call-done = bf16[1024,1024]{1,0:T(8,128)(2,1)} async-done(((bf16[256,1024]{1,0:T(8,128)(2,1)}), bf16[1024,1024]{1,0:T(8,128)(2,1)}) %all-gather.7.cloned.1.call-update) | async-done | bytes 2097168 | tf_op jit(solution)/shard_map/all_gather | solution.py:94
  129.5 14.1 %multiply_convert_fusion.1 = (bf16[1024,1024]{1,0:T(8,128)(2,1)S(1)}, f32[1024,1024]{1,0:T(8,128)}, f32[1024,1024]{1,0:T(8,128)}) fusion(f32[1024]{0:T(1024)S(1)} %convert_element_type.168, bf16[1024,1024]{1,0:T(8,128)(2,1)} %all-gather.7.cloned.1.call-done, bf16[1024,1024]{1,0:T(8,128)(2,1)S(1)} %copy-done), kind=kOutput, calls=%fused_computation.32 | convolution fusion | flops 2216689664 | bytes 14684160 | tf_op jit(solution)/shard_map/dot_general | solution.py:95
  143.6 1.4 copy-done.29
  144.9 4.3 fusion.51
  149.9 44.0 %reduce-scatter.7.cloned.1.call-done = f32[256,1024]{1,0:T(8,128)} async-done(((f32[1024,1024]{1,0:T(8,128)}), f32[256,1024]{1,0:T(8,128)}) %reduce-scatter.7.cloned.1.call-update) | async-done | bytes 1048592 | tf_op jit(solution)/shard_map/reduce_scatter | solution.py:100
  193.9 1.7 fusion.44
  196.4 1.3 fusion.43
  197.6 1.0 copy-done.9
  198.6 0.9 add_reduce_fusion.1
  199.6 22.7 %all-gather.9.cloned.1.call-done = bf16[1024,1024]{1,0:T(8,128)(2,1)} async-done(((bf16[256,1024]{1,0:T(8,128)(2,1)}), bf16[1024,1024]{1,0:T(8,128)(2,1)}) %all-gather.9.cloned.1.call-update) | async-done | bytes 2097168 | tf_op jit(solution)/shard_map/all_gather | solution.py:113
  222.3 8.3 %convert_reduce_fusion = (f32[1024]{0:T(1024)S(1)}, bf16[1024,1024]{1,0:T(8,128)(2,1)S(1)}) fusion(f32[1024,1024]{1,0:T(8,128)} %get-tuple-element.405, f32[1024,1024]{1,0:T(8,128)} %get-tuple-element.425, f32[1024]{0:T(1024)S(1)} %convert_element_type.168, bf16[1024,1024]{1,0:T(8,128)(2,1)} %all-gather.9.cloned.1.call-done, bf16[1024,1024]{1,0:T(8,128)(2,1)} %param.27), kind=kOutput, calls=%fused_computation.30 | convolution fusion | flops 2165308416 | bytes 14688256 | tf_op jit(solution)/shard_map/td,fd->tf/dot_general | solution.py:117
  230.7 1.3 copy-done.30
  232.0 4.4 fusion.52
  236.4 44.6 %reduce-scatter.9.cloned.1.call-done = f32[256,1024]{1,0:T(8,128)} async-done(((f32[1024,1024]{1,0:T(8,128)}), f32[256,1024]{1,0:T(8,128)}) %reduce-scatter.9.cloned.1.call-update) | async-done | bytes 1048592 | tf_op jit(solution)/shard_map/reduce_scatter | solution.py:123
  281.1 1.8 multiply_reduce_fusion.1
  283.3 0.9 add_reduce_fusion
  284.6 22.5 %all-gather.11.cloned.1.call-done = bf16[1024,1024]{1,0:T(8,128)(2,1)} async-done(((bf16[256,1024]{1,0:T(8,128)(2,1)}), bf16[1024,1024]{1,0:T(8,128)(2,1)}) %all-gather.11.cloned.1.call-update) | async-done | bytes 2097168 | tf_op jit(solution)/shard_map/all_gather | solution.py:135
  307.0 2.4 convolution_convert_fusion.2
  309.5 0.8 broadcast.108.clone
  310.3 20.2 %while.38 = (s32[]{:T(128)}, bf16[2,512,256]{1,2,0:T(8,128)(2,1)}, bf16[2,512,256]{2,1,0:T(8,128)(2,1)}, bf16[2,512,256]{1,2,0:T(8,128)(2,1)}, s32[2]{0:T(128)S(...) while((s32[]{:T(128)}, bf16[2,512,256]{1,2,0:T(8,128)(2,1)}, ...), condition=%wide.region_17.18_spmd, body=%wide.region_15.17_spmd.sunk | while | flops 681048064 | bytes 38854924 | solution.py:198
  313.8 0.8 fusion.123
  314.6 0.8 fusion.124
  315.4 0.9 multiply_reduce_fusion.6
  316.3 1.2 multiply_convert_fusion.3
  319.6 0.8 constant_dynamic-update-slice_fusion.8
  323.9 0.8 fusion.123
  324.7 0.8 fusion.124
  325.5 0.9 multiply_reduce_fusion.6
  326.4 1.2 multiply_convert_fusion.3
  327.6 0.8 convolution_convert_fusion.4
  329.7 0.9 constant_dynamic-update-slice_fusion.8
  330.6 1.2 copy.46
  331.8 1.2 copy.48
  333.1 5.4 convolution_bitcast_fusion
  338.8 6.7 fusion.55
  345.6 4.4 fusion.54
  350.0 1.7 fusion.53
  351.8 3.5 fusion.24
  355.3 40.4 %all-reduce = (f32[1024]{0:T(1024)}, f32[1024]{0:T(1024)}, f32[1024]{0:T(1024)}, f32[1024]{0:T(1024)}, f32[1024]{0:T(1024)}, /*index=5*/f32[1024]{0:T(1024)}) all-reduce(f32[1024]{0:T(1024)S(1)} %get-tuple-element.421, f32[1024]{0:T(1024)S(1)} %get-tuple-element.343, ...), channel_id=1, replica_groups=mesh['dp'=8,'tensor'=4] {'dp','tensor'}, use_global_device_ids=true, to_apply=%region_25.26 | all-reduce | flops 6144 | bytes 49152 | tf_op jit(solution)/shard_map/psum | solution.py:131
  395.9 23.4 %all-reduce.1 = (f32[2,256]{1,0:T(2,128)}, f32[1024]{0:T(1024)}) all-reduce(f32[2,256]{1,0:T(2,128)S(1)} %pad_maximum_fusion.3, f32[1024]{0:T(1024)S(1)} %get-tuple-element.395), channel_id=1, replica_groups=mesh['dp'=8,'tensor'=4] {'dp'}, use_global_device_ids=true, to_apply=%region_22.23 | all-reduce | flops 1536 | bytes 12288 | tf_op jit(solution)/shard_map/psum | solution.py:219
  419.3 2.4 add_add_fusion.4
  421.7 369.5 %all-reduce.5.cloned.1.call-done = (f32[3,1024,256]{1,2,0:T(8,128)}, f32[256,1024]{1,0:T(8,128)}, f32[1024,1024]{1,0:T(8,128)}, f32[1024,1024]{1,0:T(8,128)}) async-done(((f32[3,1024,256]{1,2,0:T(8,128)}, f32[256,1024]{1,0:T(8,128)}, f32[1024,1024]{1,0:T(8,128)}, f32[1024,1024]{1,0:T(8,128)}), (f32[3,1024,256]{1,2,0:T(8,128)}, f32[256,1024]{1,0:T(8,128)}, f32[1024,1024]{1,0:T(8,128)}, ...) | async-done | bytes 12582928 | tf_op jit(solution)/shard_map/psum | solution.py:219
  791.2 3.6 copy.50
  794.8 1.0 copy.98
  795.8 4.9 copy.99
  800.7 2.0 copy.100
  (138 shorter events, 13.7 us)
Async XLA Ops:
  7.2 122.3 %copy-start = (bf16[1024,1024]{1,0:T(8,128)(2,1)S(1)}, bf16[1024,1024]{1,0:T(8,128)(2,1)}, u32[]{:S(2)}) copy-start(bf16[1024,1024]{1,0:T(8,128)(2,1)} %param.25) | copy-start | bytes 6291460
  7.2 27.7 %all-gather.5.cloned.1.call-start = ((), (), s32[]{:S(2)}) async-start(), calls=%async_computation.4 | async-start | bytes 2621440 | tf_op jit(solution)/shard_map/all_gather | solution.py:41
  7.9 95.8 %reduce-scatter.5.cloned.1.call-start = ((), (), s32[]{:S(2)}) async-start(), calls=%async_computation.5 | async-start | bytes 5242880 | tf_op jit(solution)/shard_map/reduce_scatter | solution.py:83
  54.7 4.3 copy-start.2
  54.7 4.3 copy-start.4
  59.1 0.7 copy-start.19
  59.1 0.7 copy-start.20
  59.1 0.7 copy-start.21
  59.1 47.7 %copy-start.22 = (bf16[1024]{0:T(1024)(128)(2,1)S(1)}, bf16[1024]{0:T(1024)(128)(2,1)}, u32[]{:S(2)}) copy-start(bf16[1024]{0:T(1024)(128)(2,1)} %param.26) | copy-start | bytes 6148
  59.1 70.3 %all-gather.7.cloned.1.call-start = ((), (), s32[]{:S(2)}) async-start(), calls=%async_computation.6 | async-start | bytes 2621440 | tf_op jit(solution)/shard_map/all_gather | solution.py:94
  106.7 87.2 %reduce-scatter.7.cloned.1.call-start = ((), (), s32[]{:S(2)}) async-start(), calls=%async_computation.7 | async-start | bytes 5242880 | tf_op jit(solution)/shard_map/reduce_scatter | solution.py:100
  129.5 15.5 %copy-start.26 = (bf16[1024,1024]{1,0:T(8,128)(2,1)S(1)}, bf16[1024,1024]{1,0:T(8,128)(2,1)}, u32[]{:S(2)}) copy-start(bf16[1024,1024]{1,0:T(8,128)(2,1)} %param.27) | copy-start | bytes 6291460
  143.6 1.4 copy-start.29
  149.2 0.7 copy-start.23
  149.2 0.7 copy-start.24
  149.2 0.7 copy-start.25
  149.3 73.1 %all-gather.9.cloned.1.call-start = ((), (), s32[]{:S(2)}) async-start(), calls=%async_computation.8 | async-start | bytes 2621440 | tf_op jit(solution)/shard_map/all_gather | solution.py:113
  193.9 2.0 copy-start.16
  197.6 1.0 copy-start.9
  199.6 81.5 %reduce-scatter.9.cloned.1.call-start = ((), (), s32[]{:S(2)}) async-start(), calls=%async_computation.9 | async-start | bytes 5242880 | tf_op jit(solution)/shard_map/reduce_scatter | solution.py:123
  230.6 1.3 copy-start.30
  236.4 44.7 %copy-start.10 = (f32[256,1024]{1,0:T(8,128)S(1)}, f32[256,1024]{1,0:T(8,128)}, u32[]{:S(2)}) copy-start(f32[256,1024]{1,0:T(8,128)} %copy-done.9) | copy-start | bytes 3145732
  236.4 70.7 %all-gather.11.cloned.1.call-start = ((), (), s32[]{:S(2)}) async-start(), calls=%async_computation.10 | async-start | bytes 2621440 | tf_op jit(solution)/shard_map/all_gather | solution.py:135
  283.3 27.1 %copy-start.7 = (f32[256,1024]{1,0:T(8,128)}, f32[256,1024]{1,0:T(8,128)S(1)}, u32[]{:S(2)}) copy-start(f32[256,1024]{1,0:T(8,128)S(1)} %get-tuple-element.398) | copy-start | bytes 3145732
  283.3 27.0 %copy-start.3 = (bf16[1024,256]{0,1:T(8,128)(2,1)S(1)}, bf16[1024,256]{0,1:T(8,128)(2,1)}, u32[]{:S(2)}) copy-start(bf16[1024,256]{0,1:T(8,128)(2,1)} %copy-done.2) | copy-start | bytes 1572868
  283.3 27.0 %copy-start.5 = (bf16[1024,256]{0,1:T(8,128)(2,1)S(1)}, bf16[1024,256]{0,1:T(8,128)(2,1)}, u32[]{:S(2)}) copy-start(bf16[1024,256]{0,1:T(8,128)(2,1)} %copy-done.4) | copy-start | bytes 1572868
  283.3 27.0 %copy-start.6 = (bf16[1024,256]{0,1:T(8,128)(2,1)S(1)}, bf16[1024,256]{0,1:T(8,128)(2,1)}, u32[]{:S(2)}) copy-start(bf16[1024,256]{0,1:T(8,128)(2,1)} %get-tuple-element.660) | copy-start | bytes 1572868
  284.3 135.0 %reduce-scatter.11.cloned.1.call-start = ((), (), s32[]{:S(2)}) async-start(), calls=%async_computation.11 | async-start | bytes 5242880 | tf_op jit(solution)/shard_map/reduce_scatter | solution.py:212
  338.5 452.6 %all-reduce.5.cloned.1.call-start = ((), (), s32[]{:S(2)}) async-start(), calls=%async_computation.12 | async-start | bytes 25165824 | tf_op jit(solution)/shard_map/psum | solution.py:219
  338.8 6.7 copy-start.28
  338.8 6.7 copy-start.31
  345.5 4.5 copy-start.11
  345.6 4.5 copy-start.13
  345.6 6.2 copy-start.18
  345.6 6.2 copy-start.27
  355.3 40.4 %copy-start.14 = (bf16[2,512,256]{1,2,0:T(8,128)(2,1)S(1)}, bf16[2,512,256]{1,2,0:T(8,128)(2,1)}, u32[]{:S(2)}) copy-start(bf16[2,512,256]{1,2,0:T(8,128)(2,1)} %get-tuple-element.294) | copy-start | bytes 1572868
  355.3 40.4 %copy-start.15 = (bf16[2,512,256]{1,2,0:T(8,128)(2,1)S(1)}, bf16[2,512,256]{1,2,0:T(8,128)(2,1)}, u32[]{:S(2)}) copy-start(bf16[2,512,256]{1,2,0:T(8,128)(2,1)} %get-tuple-element.292) | copy-start | bytes 1572868
  355.3 64.0 %copy-start.8 = (f32[256,1024]{1,0:T(8,128)S(1)}, f32[256,1024]{1,0:T(8,128)}, u32[]{:S(2)}) copy-start(f32[256,1024]{1,0:T(8,128)} %copy-done.7) | copy-start | bytes 3145732
  791.2 3.6 copy-start.17
  795.8 4.9 copy-start.12
  795.8 7.0 copy-start.1
Sparse Core Ops, SparseCore 0:
  9.6 25.2 all-gather.4
  59.2 44.4 reduce-scatter.4
  106.8 22.5 all-gather.6
  149.4 44.5 reduce-scatter.6
  199.7 22.5 all-gather.8
  236.5 44.5 reduce-scatter.8
  284.4 22.5 all-gather.10
  338.6 45.1 reduce-scatter.10
  389.8 401.3 all-reduce.4
where the time goes:
time: 810 us; the launch traced here: 809 us
  waiting for transfers between devices  597 us (74%)
  matrix products  75.5 us (9%)
  blocking collectives  63.8 us (8%)
  local copies, waits for them, and re-layouts  33.3 us (4%)
  other arithmetic  17.9 us (2%)
  between operations  14.2 us (2%)
    psum x1, waiting for transfers between devices, on_device(): lax.psum((grad_qkv, grad_qv_bias, grad_out_weight, grad_up, grad_up_bias,...  369 us
    reduce_scatter x1, waiting for transfers between devices, on_device(): lax.psum_scatter(jnp.einsum('tf,df->td', grad_pre, up_weight, preferred_e...  44.6 us
    reduce_scatter x1, waiting for transfers between devices, on_device(): lax.psum_scatter(jnp.dot(heads_out, out_weight, preferred_element_type=jn...  44 us
    reduce_scatter x1, waiting for transfers between devices, on_device(): lax.psum_scatter(jnp.dot(hidden_low, down_weight, preferred_element_type=...  44 us
    psum x1, blocking collectives, on_device(): lax.psum((grad_gain1, grad_shift1, grad_out_bias, grad_gain2, grad_shift2...  40.4 us
    all_gather x1, waiting for transfers between devices, on_device(): gathered = lax.all_gather(tokens, 'tensor', axis=0, tiled=True)  26.2 us
    psum x1, blocking collectives, on_device(): lax.psum((grad_qkv, grad_qv_bias, grad_out_weight, grad_up, grad_up_bias,...  23.4 us
    all_gather x1, waiting for transfers between devices, on_device(): lax.all_gather(grad_second.astype(jnp.bfloat16), 'tensor', axis=0, tiled=...  22.7 us
  transfers between devices with their start and end apart: 9, of which 8 were waited for; matrix products, arithmetic and copies ran while one was open for 2% of the time, Pallas kernels for 0%

commit v1 on v0

v1 whole, which is shorter than its diff:
```python
import functools

import jax
import jax.numpy as jnp
import numpy as np
from jax import lax
from jax.experimental import pallas as pl
from jax.experimental.pallas import tpu as pltpu
from jax.sharding import PartitionSpec as P

HEAD_SIZE = 64
LENGTH = 512
EPSILON = 1e-05
BF16 = jnp.bfloat16
F32 = jnp.float32
RING = 8


def dot(a, b):
    return jnp.dot(a, b, preferred_element_type=F32)


def dot_t(a, b):
    return lax.dot_general(a, b, (((1,), (1,)), ((), ())), preferred_element_type=F32)


def dot_l(a, b):
    return lax.dot_general(a, b, (((0,), (0,)), ((), ())), preferred_element_type=F32)


def attend_kernel(first, second, weight, bias, query, key, value, mixed_first, mixed_second):
    rows = first.shape[0]
    width = query.shape[1]
    bias_wide = bias[...].astype(F32)
    for half, part in enumerate((first, second)):
        block = pl.ds(half * rows, rows)
        part = part[...]
        query[block, :] = ((dot(part, weight[0]) + bias_wide[0:1, :]) * 0.125).astype(BF16)
        key[block, :] = dot(part, weight[1]).astype(BF16)
        value[block, :] = (dot(part, weight[2]) + bias_wide[1:2, :]).astype(BF16)
    lane = lax.broadcasted_iota(jnp.int32, (rows, 128), 1)
    low_half = lane < HEAD_SIZE
    for half, mixed in enumerate((mixed_first, mixed_second)):
        block = pl.ds(half * rows, rows)
        for pair in range(width // 128):
            cols = pl.ds(pair * 128, 128)
            q_pair = query[block, cols]
            k_pair = key[:, cols]
            v_pair = value[:, cols]
            outs = []
            for side in range(2):
                keep = low_half if side == 0 else ~low_half
                scores = dot_t(jnp.where(keep, q_pair, jnp.zeros_like(q_pair)), k_pair)
                peak = jnp.max(scores, -1, keepdims=True)
                weights = jnp.exp(scores - peak)
                total = jnp.sum(weights, -1, keepdims=True)
                probs = (weights * (1.0 / total)).astype(BF16)
                outs.append(dot(probs, v_pair))
            mixed[:, cols] = jnp.where(low_half, outs[0], outs[1]).astype(BF16)


def attend(first, second, weight, bias):
    rows = first.shape[0]
    width = weight.shape[2]
    whole = jax.ShapeDtypeStruct((2 * rows, width), BF16)
    half = jax.ShapeDtypeStruct((rows, width), BF16)
    return pl.pallas_call(
        attend_kernel,
        out_shape=(whole, whole, whole, half, half),
        compiler_params=pltpu.CompilerParams(vmem_limit_bytes=40 * 2**20),
        cost_estimate=pl.CostEstimate(
            flops=2 * 2 * rows * first.shape[1] * width * 3 + 16 * rows * rows * width * 4,
            bytes_accessed=6 * 2**20,
            transcendentals=0,
        ),
    )(first, second, weight, bias)


def attend_back_kernel(query, key, value, grad_first, grad_second, out, key_sum, value_sum):
    rows = grad_first.shape[0]
    width = query.shape[1]
    lane = lax.broadcasted_iota(jnp.int32, (rows, 128), 1)
    low_half = lane < HEAD_SIZE
    lane_all = lax.broadcasted_iota(jnp.int32, (2 * rows, 128), 1)
    low_all = lane_all < HEAD_SIZE
    for pair in range(width // 128):
        cols = pl.ds(pair * 128, 128)
        k_pair = key[:, cols]
        v_pair = value[:, cols]
        for half, grads in enumerate((grad_first, grad_second)):
            block = pl.ds(half * rows, rows)
            q_pair = query[block, cols]
            g_pair = grads[:, cols]
            dq, dk, dv = [], [], []
            for side in range(2):
                keep = low_half if side == 0 else ~low_half
                scores = dot_t(jnp.where(keep, q_pair, jnp.zeros_like(q_pair)), k_pair)
                peak = jnp.max(scores, -1, keepdims=True)
                weights = jnp.exp(scores - peak)
                total = jnp.sum(weights, -1, keepdims=True)
                probs = weights * (1.0 / total)
                grad_probs = dot_t(jnp.where(keep, g_pair, jnp.zeros_like(g_pair)), v_pair)
                inner = probs * grad_probs
                grad_scores = (
                    inner - probs * jnp.sum(inner, -1, keepdims=True)
                ).astype(BF16)
                dv.append(dot_l(probs.astype(BF16), g_pair))
                dq.append(dot(grad_scores, k_pair))
                dk.append(dot_l(grad_scores, q_pair))
            out[0, block, cols] = (
                jnp.where(low_half, dq[0], dq[1]).astype(BF16).astype(F32) * 0.125
            ).astype(BF16)
            dk_pair = jnp.where(low_all, dk[0], dk[1])
            dv_pair = jnp.where(low_all, dv[0], dv[1])
            if half == 0:
                key_sum[...] = dk_pair
                value_sum[...] = dv_pair
            else:
                out[1, :, cols] = (key_sum[...] + dk_pair).astype(BF16)
                out[2, :, cols] = (value_sum[...] + dv_pair).astype(BF16)


def attend_back(query, key, value, grad_first, grad_second):
    length, width = query.shape
    return pl.pallas_call(
        attend_back_kernel,
        out_shape=jax.ShapeDtypeStruct((3, length, width), BF16),
        scratch_shapes=[pltpu.VMEM((length, 128), F32), pltpu.VMEM((length, 128), F32)],
        compiler_params=pltpu.CompilerParams(vmem_limit_bytes=40 * 2**20),
        cost_estimate=pl.CostEstimate(
            flops=4 * length * length * width * 2 * 5,
            bytes_accessed=2 * 2**20,
            transcendentals=0,
        ),
    )(query, key, value, grad_first, grad_second)


def center_scale(values):
    center = values - jnp.mean(values, -1, keepdims=True)
    spread = jnp.mean(center * center, -1, keepdims=True)
    scale = lax.rsqrt(spread + EPSILON)
    return center * scale, scale


def norm_back(grad, unit, scale, gain):
    grad_unit = grad * gain
    return scale * (
        grad_unit
        - jnp.mean(grad_unit, -1, keepdims=True)
        - unit * jnp.mean(grad_unit * unit, -1, keepdims=True)
    )


def gate(pre):
    cdf = 0.5 * (1.0 + lax.erf(pre * np.float32(np.sqrt(0.5))))
    return pre * cdf


def gate_slope(pre):
    cdf = 0.5 * (1.0 + lax.erf(pre * np.float32(np.sqrt(0.5))))
    return cdf + pre * (np.float32(1 / np.sqrt(2 * np.pi)) * jnp.exp(-0.5 * pre * pre))


def swap(values, bit, tensor):
    return lax.ppermute(values, "tensor", [(i, i ^ bit) for i in range(tensor)])


def ring_sum(grad, dp, forward):
    order = list(range(0, dp, 2)) + list(range(dp - 1, 0, -2))
    place = [0] * dp
    for at, device in enumerate(order):
        place[device] = at
    pairs = [(order[i], order[(i + 1) % dp]) for i in range(dp)]
    sign = 1
    if not forward:
        pairs = [(b, a) for a, b in pairs]
        sign = -1
    pos = jnp.asarray(np.array(place, np.int32))[lax.axis_index("dp")]
    rows, columns = grad.shape[0] // dp, grad.shape[1]

    def chunk(step):
        first = lax.rem(pos + (sign * step) % dp, dp) * rows
        return first

    def own(step):
        return lax.dynamic_slice(grad, (chunk(step), 0), (rows, columns))

    moving = own(0).astype(BF16)
    for step in range(1, dp):
        moving = lax.ppermute(moving, "dp", pairs)
        moving = (moving.astype(F32) + own(-step)).astype(BF16)
    out = jnp.zeros(grad.shape, F32)
    out = lax.dynamic_update_slice(out, moving.astype(F32), (chunk(1), 0))
    for step in range(1, dp):
        moving = lax.ppermute(moving, "dp", pairs)
        out = lax.dynamic_update_slice(out, moving.astype(F32), (chunk(1 - step), 0))
    return out


def dp_sum(grad, dp):
    if dp != RING:
        return lax.psum(grad, "dp")
    half = grad.shape[0] // 2
    return jnp.concatenate([ring_sum(grad[:half], dp, True), ring_sum(grad[half:], dp, False)], 0)


def cube_sum(values, axis, size):
    bit = 1
    while bit < size:
        values = values + lax.ppermute(values, axis, [(i, i ^ bit) for i in range(size)])
        bit *= 2
    return values


def on_device(
    dp,
    tensor,
    tokens,
    qkv_weight,
    qv_bias,
    out_weight,
    out_bias,
    norm1_gain,
    norm1_bias,
    up_weight,
    up_bias,
    down_weight,
    down_bias,
    norm2_gain,
    norm2_bias,
    cotangent,
):
    core = functools.partial(swap, bit=1, tensor=tensor)
    chip = functools.partial(swap, bit=2, tensor=tensor)
    rows, model = tokens.shape
    tok_a = tokens
    tok_c = chip(tok_a)
    tok_b = core(tok_a)
    out_peer = core(out_weight)
    up_peer = core(up_weight)
    down_peer = core(down_weight)
    up_bias_peer = core(up_bias)
    qkv_peer = core(qkv_weight)
    gain1, shift1 = norm1_gain.astype(F32), norm1_bias.astype(F32)
    gain2, shift2 = norm2_gain.astype(F32), norm2_bias.astype(F32)

    q_ab, k_ab, v_ab, mix_a, mix_b = attend(tok_a, tok_b, qkv_weight, qv_bias)
    sum_a = dot(mix_a, out_weight) + dot(core(mix_b), out_peer)
    tok_d = core(tok_c)
    q_cd, k_cd, v_cd, mix_c, mix_d = attend(tok_c, tok_d, qkv_weight, qv_bias)
    sum_c = dot(mix_c, out_weight) + dot(core(mix_d), out_peer)
    low_a, low_c = sum_a.astype(BF16), sum_c.astype(BF16)
    far_c = chip(low_a)
    far_a = chip(low_c)
    out_bias_wide = out_bias.astype(F32)
    first_a = tok_a.astype(F32) + low_a.astype(F32) + far_a.astype(F32) + out_bias_wide
    first_c = tok_c.astype(F32) + low_c.astype(F32) + far_c.astype(F32) + out_bias_wide
    unit1_a, scale1_a = center_scale(first_a)
    unit1_c, _ = center_scale(first_c)
    normed_a = unit1_a * gain1 + shift1
    nrm_a = normed_a.astype(BF16)
    nrm_c = (unit1_c * gain1 + shift1).astype(BF16)

    up_bias_wide = up_bias.astype(F32)
    up_bias_peer_wide = up_bias_peer.astype(F32)

    def feed(nrm):
        pre = dot(nrm, up_weight) + up_bias_wide
        pre_peer = dot(nrm, up_peer) + up_bias_peer_wide
        act, act_peer = gate(pre).astype(BF16), gate(pre_peer).astype(BF16)
        return pre, pre_peer, act, act_peer, dot(act, down_weight) + dot(act_peer, down_peer)

    pre_c, pre_peer_c, act_c, act_peer_c, feed_c = feed(nrm_c)
    far_feed = chip(feed_c.astype(BF16))
    pre_a, pre_peer_a, act_a, act_peer_a, feed_a = feed(nrm_a)
    second_a = normed_a + feed_a + far_feed.astype(F32) + down_bias.astype(F32)
    unit2, scale2 = center_scale(second_a)
    layer_out = (unit2 * gain2 + shift2).astype(BF16)
    cot = cotangent.astype(F32)
    grad_second = norm_back(cot, unit2, scale2, gain2)
    gs_a = grad_second.astype(BF16)
    gs_c = chip(gs_a)
    gs_b, gs_d = core(gs_a), core(gs_c)
    act_b, act_d = core(act_peer_a), core(act_peer_c)
    nrm_b, nrm_d = core(nrm_a), core(nrm_c)

    def stack(*parts):
        return jnp.concatenate(parts, 0)

    def feed_back(gs, pre, pre_peer):
        gp = (gate_slope(pre) * dot_t(gs, down_weight)).astype(BF16)
        gp_peer = (gate_slope(pre_peer) * dot_t(gs, down_peer)).astype(BF16)
        return gp, gp_peer, dot_t(gp, up_weight) + dot_t(gp_peer, up_peer)

    gp_c, gp_peer_c, back_c = feed_back(gs_c, pre_c, pre_peer_c)
    far_back = chip(back_c.astype(BF16))
    gp_a, gp_peer_a, back_a = feed_back(gs_a, pre_a, pre_peer_a)
    gp_b, gp_d = core(gp_peer_a), core(gp_peer_c)
    grad_down = dot_l(stack(act_a, act_b, act_c, act_d), stack(gs_a, gs_b, gs_c, gs_d))
    grad_down = dp_sum(grad_down, dp)
    gp_all = stack(gp_a, gp_b, gp_c, gp_d)
    grad_up = dot_l(stack(nrm_a, nrm_b, nrm_c, nrm_d), gp_all)
    grad_up = dp_sum(grad_up, dp)
    grad_up_bias = jnp.sum(gp_all.astype(F32), 0)

    grad_normed = grad_second + back_a + far_back.astype(F32)
    grad_first = norm_back(grad_normed, unit1_a, scale1_a, gain1)
    gf_a = grad_first.astype(BF16)
    gf_c = chip(gf_a)
    gf_b, gf_d = core(gf_a), core(gf_c)

    def heads_back(gf):
        return dot_t(gf, out_weight).astype(BF16), dot_t(gf, out_peer).astype(BF16)

    gh_a, gh_peer_a = heads_back(gf_a)
    gp_ab = attend_back(q_ab, k_ab, v_ab, gh_a, core(gh_peer_a))
    gh_c, gh_peer_c = heads_back(gf_c)
    gp_cd = attend_back(q_cd, k_cd, v_cd, gh_c, core(gh_peer_c))
    grad_out = dot_l(stack(mix_a, mix_b, mix_c, mix_d), stack(gf_a, gf_b, gf_c, gf_d))

    def proj_back(grads):
        near, far = grads[:, :rows], core(grads[:, rows:])
        total = 0.0
        for i in range(3):
            total = total + dot_t(near[i], qkv_weight[i]) + dot_t(far[i], qkv_peer[i])
        return total

    rows_c = proj_back(gp_cd)
    far_rows = chip(rows_c.astype(BF16))
    token_grad = grad_first + proj_back(gp_ab) + far_rows.astype(F32)
    tok_all = stack(tok_a, tok_b, tok_c, tok_d)
    proj_all = jnp.concatenate([gp_ab, gp_cd], 1)
    grad_qkv = jnp.concatenate([dot_l(tok_all, proj_all[i]) for i in range(3)], 0)
    grad_qkv = dp_sum(grad_qkv, dp).reshape(qkv_weight.shape)
    grad_out = dp_sum(grad_out, dp)
    grad_qv_bias = jnp.sum(proj_all.astype(F32), 1)

    small = jnp.stack(
        [
            jnp.sum(grad_normed * unit1_a, 0),
            jnp.sum(grad_normed, 0),
            jnp.sum(grad_first, 0),
            jnp.sum(cot * unit2, 0),
            jnp.sum(cot, 0),
            jnp.sum(grad_second, 0),
        ]
    )
    small = cube_sum(small, "tensor", tensor)
    flat = jnp.concatenate(
        [small.reshape(-1), grad_up_bias, grad_qv_bias[0], grad_qv_bias[2]]
    )
    flat = cube_sum(flat.reshape(-1, 128), "dp", dp).reshape(-1)
    small = flat[: 6 * model].reshape(6, model)
    hidden = grad_up_bias.shape[0]
    grad_up_bias = flat[6 * model : 6 * model + hidden]
    grad_qv = flat[6 * model + hidden :].reshape(2, -1)
    return (
        layer_out,
        token_grad,
        grad_qkv,
        grad_qv,
        grad_out,
        small[2],
        small[0],
        small[1],
        grad_up,
        grad_up_bias,
        grad_down,
        small[5],
        small[3],
        small[4],
    )


def solution(mesh):
    dp, tensor = mesh.shape["dp"], mesh.shape["tensor"]
    placed = (
        P(("dp", "tensor"), None),
        P(None, None, "tensor"),
        P(None, "tensor"),
        P("tensor", None),
        P(),
        P(),
        P(),
        P(None, "tensor"),
        P("tensor"),
        P("tensor", None),
        P(),
        P(),
        P(),
        P(("dp", "tensor"), None),
    )
    return jax.shard_map(
        functools.partial(on_device, dp, tensor),
        mesh=mesh,
        in_specs=placed,
        out_specs=(
            P(("dp", "tensor"), None),
            P(("dp", "tensor"), None),
            P(None, None, "tensor"),
            P(None, "tensor"),
            P("tensor", None),
            P(),
            P(),
            P(),
            P(None, "tensor"),
            P("tensor"),
            P("tensor", None),
            P(),
            P(),
            P(),
        ),
        check_vma=False,
    )
```

time: 810 us -> 539 us (0.67); the launches traced: 809 us -> 529 us
  waiting for transfers between devices: 597 us -> 214 us
  starting transfers between devices: 1.03 us -> 144 us
  blocking collectives: 63.8 us -> 0 us
  other arithmetic: 17.9 us -> 39.1 us
  Pallas kernels: 0 us -> 20 us
  local copies, waits for them, and re-layouts: 33.3 us -> 19.1 us
    psum x1 -> x0, waiting for transfers between devices: 369 us -> none  [on_device(): lax.psum((grad_qkv, grad_qv_bias, grad_out_weight, grad_up, grad_up_bias,...]
    ppermute x0 -> x148, waiting for transfers between devices: none -> 214 us  [the longest x112 170 us: ring_sum(): moving = lax.ppermute(moving, 'dp', pairs)]
    ppermute x0 -> x148, starting transfers between devices: none -> 144 us  [the longest x112 123 us: ring_sum(): moving = lax.ppermute(moving, 'dp', pairs)]
    reduce_scatter x4 -> x0, waiting for transfers between devices: 133 us -> none  [the longest x1 44.6 us: on_device(): lax.psum_scatter(jnp.einsum('tf,df->td', grad_pre, up_weight, preferred_e...]
    all_gather x4 -> x0, waiting for transfers between devices: 94 us -> none  [the longest x1 26.2 us: on_device(): gathered = lax.all_gather(tokens, 'tensor', axis=0, tiled=True)]
    psum x2 -> x0, blocking collectives: 63.8 us -> none  [the longest x1 40.4 us: on_device(): lax.psum((grad_gain1, grad_shift1, grad_out_bias, grad_gain2, grad_shift2...]
    pallas_call x0 -> x4, Pallas kernels: none -> 20 us  [the longest x2 10.9 us: attend_back(): pl.pallas_call(attend_back_kernel, out_shape=jax.ShapeDtypeStruct((3, len...]
    convert_element_type x11 -> x58, other arithmetic: 4.47 us -> 19.6 us  [the longest x46 10.9 us: ring_sum(): moving = (moving.astype(F32) + own(-step)).astype(BF16)]
  transfers between devices with their start and end apart: 9 -> 148, of which waited for: 8 -> 69; matrix products, arithmetic and copies ran while one was open for 2% -> 25% of each run, Pallas kernels for 0% -> 4%
where the time goes in v1:
time: 539 us; the launch traced here: 529 us
  waiting for transfers between devices  214 us (40%)
  starting transfers between devices  144 us (27%)
  matrix products  82.6 us (15%)
  other arithmetic  39.1 us (7%)
  Pallas kernels  20 us (4%)
  local copies, waits for them, and re-layouts  19.1 us (4%)
  between operations  9.64 us (2%)
    ppermute x112, waiting for transfers between devices, ring_sum(): moving = lax.ppermute(moving, 'dp', pairs)  170 us
    ppermute x112, starting transfers between devices, ring_sum(): moving = lax.ppermute(moving, 'dp', pairs)  123 us
    dot_general x24, matrix products, dot_t(): lax.dot_general(a, b, (((1,), (1,)), ((), ())), preferred_element_type=F32)  46.3 us
    ppermute x31, waiting for transfers between devices, swap(): return lax.ppermute(values, 'tensor', [(i, i ^ bit) for i in range(tensor)])  34.2 us
    dot_general x12, matrix products, dot(): return jnp.dot(a, b, preferred_element_type=F32)  24.5 us
    ppermute x31, starting transfers between devices, swap(): return lax.ppermute(values, 'tensor', [(i, i ^ bit) for i in range(tensor)])  13.5 us
    dot_general x6, matrix products, dot_l(): lax.dot_general(a, b, (((0,), (0,)), ((), ())), preferred_element_type=F32)  11.8 us
    convert_element_type x46, other arithmetic, ring_sum(): moving = (moving.astype(F32) + own(-step)).astype(BF16)  10.9 us
  transfers between devices with their start and end apart: 148, of which 69 were waited for; matrix products, arithmetic and copies ran while one was open for 25% of the time, Pallas kernels for 4%

profile of v1, /device:TPU:0, one launch (start us, length us, event | category | flops | bytes accessed | tf_op | source)
XLA Modules:
  0.0 528.7 jit_solution(7478904251486165571)
XLA Ops:
  7.0 4.6 shard_map.317
  12.1 4.4 collective-permute-done.3.first
  19.0 4.6 shard_map.318
  25.4 6.2 %collective-permute-done.10 = bf16[256,1024]{1,0:T(8,128)(2,1)S(1)} collective-permute-done((bf16[256,1024]{1,0:T(8,128)(2,1)S(1)}, bf16[256,1024]{1,0:T(8,128)(2,1)S(1)}, u32[]{:S(2)}, u32[]{:S(2)}) %collective-permute-start.10) | collective-permute-done | bytes 524320 | tf_op jit(solution)/shard_map/ppermute | solution.py:165
  63.5 3.6 multiply_convert_fusion
  72.2 3.2 multiply_convert_fusion.2
  75.5 8.0 %collective-permute-done.11 = bf16[256,1024]{1,0:T(8,128)(2,1)S(1)} collective-permute-done((bf16[256,1024]{1,0:T(8,128)(2,1)S(1)}, bf16[256,1024]{1,0:T(8,128)(2,1)S(1)}, u32[]{:S(2)}, u32[]{:S(2)}) %collective-permute-start.11) | collective-permute-done | bytes 524320 | tf_op jit(solution)/shard_map/ppermute | solution.py:165
  83.5 2.8 fusion.186
  91.7 2.7 fusion.69
  94.5 8.0 %collective-permute-done.12 = bf16[256,1024]{1,0:T(8,128)(2,1)} collective-permute-done((bf16[256,1024]{1,0:T(8,128)(2,1)}, bf16[256,1024]{1,0:T(8,128)(2,1)}, u32[]{:S(2)}, u32[]{:S(2)}) %collective-permute-start.12) | collective-permute-done | bytes 524320 | tf_op jit(solution)/shard_map/ppermute | solution.py:165
  102.6 2.8 fusion.51
  107.9 2.7 fusion.79
  113.3 2.7 fusion.50
  118.6 6.5 %collective-permute-done.13 = bf16[256,1024]{1,0:T(8,128)(2,1)S(1)} collective-permute-done((bf16[256,1024]{1,0:T(8,128)(2,1)S(1)}, bf16[256,1024]{1,0:T(8,128)(2,1)S(1)}, u32[]{:S(2)}, u32[]{:S(2)}) %collective-permute-start.13) | collective-permute-done | bytes 524320 | tf_op jit(solution)/shard_map/ppermute | solution.py:165
  125.1 2.8 multiply_reduce_fusion
  129.9 2.8 fusion.8
  140.1 4.5 fusion.16
  149.6 4.5 collective-permute-done.50
  157.9 5.4 %shard_map.319 = bf16[3,512,256]{2,1,0:T(8,128)(2,1)S(1)} custom-call(bf16[512,256]{1,0:T(8,128)(2,1)S(1)} %copy-done.17, bf16[512,256]{1,0:T(8,128)(2,1)S(1)} %copy-done.19, bf16[512,256]{1,0:T(8,128)(2,1)S(1)} %copy-done.21, bf16[256,256]{1,0:T(8,128)(2,1)S(1)} %convolution_convert_fusion.3.grad_first, bf16[256,256]{1,0:T(8,128)(2,1)S(1)} %collective-permute-done.14.grad_second), custom_call_target="tpu_custom_call" | custom-call | flops 2684354560 | bytes 2097152 | tf_op jit(solution)/shard_map/pallas_call | solution.py:125
  172.8 3.2 collective-permute-done.120
  177.6 4.6 collective-permute-done.103
  183.4 3.8 collective-permute-done.135
  188.8 3.3 collective-permute-done.89
  193.7 3.4 collective-permute-done.121
  198.3 3.8 collective-permute-done.104
  203.3 3.8 collective-permute-done.136
  208.6 3.4 collective-permute-done.90
  213.6 3.4 collective-permute-done.122
  235.6 5.4 %shard_map.320 = bf16[3,512,256]{2,1,0:T(8,128)(2,1)S(1)} custom-call(bf16[512,256]{1,0:T(8,128)(2,1)S(1)} %copy-done.11, bf16[512,256]{1,0:T(8,128)(2,1)S(1)} %copy-done.13, bf16[512,256]{1,0:T(8,128)(2,1)S(1)} %copy-done.15, bf16[256,256]{1,0:T(8,128)(2,1)S(1)} %convolution_convert_fusion.1.grad_first, bf16[256,256]{1,0:T(8,128)(2,1)S(1)} %collective-permute-done.18.grad_second), custom_call_target="tpu_custom_call" | custom-call | flops 2684354560 | bytes 2097152 | tf_op jit(solution)/shard_map/pallas_call | solution.py:125
  258.1 2.7 collective-permute-start.55
  268.0 2.9 collective-permute-done.107
  272.5 3.3 collective-permute-done.93
  278.1 2.8 collective-permute-done.139
  282.5 3.3 collective-permute-done.125
  287.4 3.0 collective-permute-done.22
  291.9 4.3 collective-permute-done.108
  298.9 3.1 collective-permute-done.94
  309.3 3.1 collective-permute-done.126
  314.2 2.8 collective-permute-done.23
  337.8 3.3 collective-permute-done.73
  346.4 2.7 collective-permute-done.74
  355.1 3.6 collective-permute-done.75
  373.6 4.2 collective-permute-done.77
  378.8 3.2 collective-permute-done.63
  389.7 2.7 collective-permute-done.64
  393.5 2.9 collective-permute-done.79
  397.5 2.8 collective-permute-done.65
  412.9 3.5 collective-permute-done.81
  417.2 3.0 collective-permute-done.67
  421.2 3.3 collective-permute-done.82
  425.4 3.4 collective-permute-done.68
  429.7 3.3 collective-permute-done.83
  433.8 3.0 collective-permute-done.69
  437.7 3.7 collective-permute-done.28
  442.5 3.6 collective-permute-done.37
  454.8 4.7 collective-permute-done.85
  460.0 3.3 collective-permute-done.71
  483.5 3.1 collective-permute-done.41
  487.3 4.0 collective-permute-done.32
  504.8 3.1 collective-permute-done.44
  509.3 3.1 collective-permute-done.45
  514.0 3.1 collective-permute-done.46
  518.6 3.1 collective-permute-done.47
  523.2 3.1 collective-permute-done.48
  (615 shorter events, 284.2 us)
Async XLA Ops:
  1.2 15.3 %collective-permute-start.3 = (bf16[256,1024]{1,0:T(8,128)(2,1)}, bf16[256,1024]{1,0:T(8,128)(2,1)S(1)}, u32[]{:S(2)}, u32[]{:S(2)}) collective-permute-start(bf16[256,1024]{1,0:T(8,128)(2,1)} %first.1), channel_id=1, source_target_pairs={{0,2},{1,3},{2,0},{3,1},{4,6},{5,7},{6,4},{7,5},{8,10},{9,11},{10,... | collective-permute-start | bytes 1572872 | tf_op jit(solution)/shard_map/ppermute | solution.py:165
  3.7 12.7 %collective-permute-start.2 = (bf16[256,1024]{1,0:T(8,128)(2,1)}, bf16[256,1024]{1,0:T(8,128)(2,1)S(1)}, u32[]{:S(2)}, u32[]{:S(2)}) collective-permute-start(bf16[256,1024]{1,0:T(8,128)(2,1)} %param.25), channel_id=1, source_target_pairs={{0,1},{1,0},{2,3},{3,2},{4,5},{5,4},{6,7},{7,6},{8,9},{9,8},{10,11... | collective-permute-start | bytes 1572872 | tf_op jit(solution)/shard_map/ppermute | solution.py:165
  17.1 14.4 %collective-permute-start.10 = (bf16[256,1024]{1,0:T(8,128)(2,1)S(1)}, bf16[256,1024]{1,0:T(8,128)(2,1)S(1)}, u32[]{:S(2)}, u32[]{:S(2)}) collective-permute-start(bf16[256,1024]{1,0:T(8,128)(2,1)S(1)} %fusion.53), channel_id=1, source_target_pairs={{0,2},{1,3},{2,0},{3,1},{4,6},{5,7},{6,4},{7,5},{8,10},{9,11},{10,... | collective-permute-start | bytes 1572872 | tf_op jit(solution)/shard_map/ppermute | solution.py:165
  33.4 18.6 %collective-permute-start.6 = (bf16[256,1024]{1,0:T(8,128)(2,1)}, bf16[256,1024]{1,0:T(8,128)(2,1)}, u32[]{:S(2)}, u32[]{:S(2)}) collective-permute-start(bf16[256,1024]{1,0:T(8,128)(2,1)} %get-tuple-element.89), channel_id=1, source_target_pairs={{0,2},{1,3},{2,0},{3,1},{4,6},{5,7},{6,4},{7,5},{8,10},{9,11},{10,... | collective-permute-start | bytes 1572872 | tf_op jit(solution)/shard_map/ppermute | solution.py:165
  35.2 186.7 %collective-permute-start.16 = (bf16[3,1024,256]{2,1,0:T(8,128)(2,1)S(1)}, bf16[3,1024,256]{2,1,0:T(8,128)(2,1)}, u32[]{:S(2)}, u32[]{:S(2)}) collective-permute-start(bf16[3,1024,256]{2,1,0:T(8,128)(2,1)S(1)} %copy-done.1), channel_id=1, source_target_pairs={{0,1},{1,0},{2,3},{3,2},{4,5},{5,4},{6,7},{7,6},{8,9},{9,8},{10,11... | collective-permute-start | bytes 4718600 | tf_op jit(solution)/shard_map/ppermute | solution.py:165
  35.2 13.6 %collective-permute-start.8 = (bf16[1024]{0:T(1024)(128)(2,1)}, bf16[1024]{0:T(1024)(128)(2,1)}, u32[]{:S(2)}, u32[]{:S(2)}) collective-permute-start(bf16[1024]{0:T(1024)(128)(2,1)} %param.30), channel_id=1, source_target_pairs={{0,1},{1,0},{2,3},{3,2},{4,5},{5,4},{6,7},{7,6},{8,9},{9,8},{10,11... | collective-permute-start | bytes 6152 | tf_op jit(solution)/shard_map/ppermute | solution.py:165
  35.7 27.8 %collective-permute-start.7 = (bf16[1024,1024]{1,0:T(8,128)(2,1)}, bf16[1024,1024]{1,0:T(8,128)(2,1)}, u32[]{:S(2)}, u32[]{:S(2)}) collective-permute-start(bf16[1024,1024]{1,0:T(8,128)(2,1)} %param.29), channel_id=1, source_target_pairs={{0,1},{1,0},{2,3},{3,2},{4,5},{5,4},{6,7},{7,6},{8,9},{9,8},{10,11... | collective-permute-start | bytes 6291464 | tf_op jit(solution)/shard_map/ppermute | solution.py:165
  35.7 31.4 %collective-permute-start.9 = (bf16[1024,1024]{1,0:T(8,128)(2,1)}, bf16[1024,1024]{1,0:T(8,128)(2,1)}, u32[]{:S(2)}, u32[]{:S(2)}) collective-permute-start(bf16[1024,1024]{1,0:T(8,128)(2,1)} %param.31), channel_id=1, source_target_pairs={{0,1},{1,0},{2,3},{3,2},{4,5},{5,4},{6,7},{7,6},{8,9},{9,8},{10,11... | collective-permute-start | bytes 6291464 | tf_op jit(solution)/shard_map/ppermute | solution.py:165
  69.6 13.9 %collective-permute-start.11 = (bf16[256,1024]{1,0:T(8,128)(2,1)S(1)}, bf16[256,1024]{1,0:T(8,128)(2,1)S(1)}, u32[]{:S(2)}, u32[]{:S(2)}) collective-permute-start(bf16[256,1024]{1,0:T(8,128)(2,1)S(1)} %fusion.49), channel_id=1, source_target_pairs={{0,2},{1,3},{2,0},{3,1},{4,6},{5,7},{6,4},{7,5},{8,10},{9,11},{10,... | collective-permute-start | bytes 1572872 | tf_op jit(solution)/shard_map/ppermute | solution.py:165
  89.3 13.3 %collective-permute-start.12 = (bf16[256,1024]{1,0:T(8,128)(2,1)}, bf16[256,1024]{1,0:T(8,128)(2,1)}, u32[]{:S(2)}, u32[]{:S(2)}) collective-permute-start(bf16[256,1024]{1,0:T(8,128)(2,1)} %convert_element_type.704), channel_id=1, source_target_pairs={{0,2},{1,3},{2,0},{3,1},{4,6},{5,7},{6,4},{7,5},{8,10},{9,11},{10,... | collective-permute-start | bytes 1572872 | tf_op jit(solution)/shard_map/ppermute | solution.py:165
  91.2 36.7 %collective-permute-start.87 = (bf16[256,1024]{1,0:T(8,128)(2,1)S(1)}, bf16[256,1024]{1,0:T(8,128)(2,1)S(1)}, u32[]{:S(2)}, u32[]{:S(2)}) collective-permute-start(bf16[256,1024]{1,0:T(8,128)(2,1)S(1)} %get-tuple-element.83), channel_id=1, source_target_pairs={{0,1},{1,0},{2,3},{3,2},{4,5},{5,4},{6,7},{7,6},{8,9},{9,8},{10,11... | collective-permute-start | bytes 1572872 | tf_op jit(solution)/shard_map/ppermute | solution.py:165
  91.2 37.3 %collective-permute-start.86 = (bf16[256,1024]{1,0:T(8,128)(2,1)S(1)}, bf16[256,1024]{1,0:T(8,128)(2,1)S(1)}, u32[]{:S(2)}, u32[]{:S(2)}) collective-permute-start(bf16[256,1024]{1,0:T(8,128)(2,1)S(1)} %get-tuple-element.84), channel_id=1, source_target_pairs={{0,1},{1,0},{2,3},{3,2},{4,5},{5,4},{6,7},{7,6},{8,9},{9,8},{10,11... | collective-permute-start | bytes 1572872 | tf_op jit(solution)/shard_map/ppermute | solution.py:165
  94.5 34.2 %collective-permute-start.51 = (bf16[256,1024]{1,0:T(8,128)(2,1)S(1)}, bf16[256,1024]{1,0:T(8,128)(2,1)S(1)}, u32[]{:S(2)}, u32[]{:S(2)}) collective-permute-start(bf16[256,1024]{1,0:T(8,128)(2,1)S(1)} %fusion.69), channel_id=1, source_target_pairs={{0,1},{1,0},{2,3},{3,2},{4,5},{5,4},{6,7},{7,6},{8,9},{9,8},{10,11... | collective-permute-start | bytes 1572872 | tf_op jit(solution)/shard_map/ppermute | solution.py:165
  113.0 12.1 %collective-permute-start.13 = (bf16[256,1024]{1,0:T(8,128)(2,1)S(1)}, bf16[256,1024]{1,0:T(8,128)(2,1)S(1)}, u32[]{:S(2)}, u32[]{:S(2)}) collective-permute-start(bf16[256,1024]{1,0:T(8,128)(2,1)S(1)} %fusion.52), channel_id=1, source_target_pairs={{0,2},{1,3},{2,0},{3,1},{4,6},{5,7},{6,4},{7,5},{8,10},{9,11},{10,... | collective-permute-start | bytes 1572872 | tf_op jit(solution)/shard_map/ppermute | solution.py:165
  128.0 11.1 %collective-permute-start.117 = (bf16[256,1024]{1,0:T(8,128)(2,1)}, bf16[256,1024]{1,0:T(8,128)(2,1)}, u32[]{:S(2)}, u32[]{:S(2)}) collective-permute-start(bf16[256,1024]{1,0:T(8,128)(2,1)} %get-tuple-element.96), channel_id=1, source_target_pairs={{0,1},{1,0},{2,3},{3,2},{4,5},{5,4},{6,7},{7,6},{8,9},{9,8},{10,11... | collective-permute-start | bytes 1572872 | tf_op jit(solution)/shard_map/ppermute | solution.py:165
  128.5 10.9 %collective-permute-start.116 = (bf16[256,1024]{1,0:T(8,128)(2,1)}, bf16[256,1024]{1,0:T(8,128)(2,1)}, u32[]{:S(2)}, u32[]{:S(2)}) collective-permute-start(bf16[256,1024]{1,0:T(8,128)(2,1)} %get-tuple-element.92), channel_id=1, source_target_pairs={{0,1},{1,0},{2,3},{3,2},{4,5},{5,4},{6,7},{7,6},{8,9},{9,8},{10,11... | collective-permute-start | bytes 1572872 | tf_op jit(solution)/shard_map/ppermute | solution.py:165
  128.6 10.8 %collective-permute-start.118 = (bf16[256,1024]{1,0:T(8,128)(2,1)}, bf16[256,1024]{1,0:T(8,128)(2,1)}, u32[]{:S(2)}, u32[]{:S(2)}) collective-permute-start(bf16[256,1024]{1,0:T(8,128)(2,1)} %convert_element_type.704), channel_id=1, source_target_pairs={{0,1},{1,0},{2,3},{3,2},{4,5},{5,4},{6,7},{7,6},{8,9},{9,8},{10,11... | collective-permute-start | bytes 1572872 | tf_op jit(solution)/shard_map/ppermute | solution.py:165
  129.1 10.9 %collective-permute-start.119 = (bf16[256,1024]{1,0:T(8,128)(2,1)}, bf16[256,1024]{1,0:T(8,128)(2,1)}, u32[]{:S(2)}, u32[]{:S(2)}) collective-permute-start(bf16[256,1024]{1,0:T(8,128)(2,1)} %collective-permute-done.12), channel_id=1, source_target_pairs={{0,1},{1,0},{2,3},{3,2},{4,5},{5,4},{6,7},{7,6},{8,9},{9,8},{10,11... | collective-permute-start | bytes 1572872 | tf_op jit(solution)/shard_map/ppermute | solution.py:165
  139.1 79.2 %collective-permute-start.17 = (bf16[256,1024]{1,0:T(8,128)(2,1)}, bf16[256,1024]{1,0:T(8,128)(2,1)}, u32[]{:S(2)}, u32[]{:S(2)}) collective-permute-start(bf16[256,1024]{1,0:T(8,128)(2,1)} %convert_element_type.711), channel_id=1, source_target_pairs={{0,2},{1,3},{2,0},{3,1},{4,6},{5,7},{6,4},{7,5},{8,10},{9,11},{10,... | collective-permute-start | bytes 1572872 | tf_op jit(solution)/shard_map/ppermute | solution.py:165
  139.5 178.6 %collective-permute-start.56 = (bf16[256,1024]{1,0:T(8,128)(2,1)}, bf16[256,1024]{1,0:T(8,128)(2,1)}, u32[]{:S(2)}, u32[]{:S(2)}) collective-permute-start(bf16[256,1024]{1,0:T(8,128)(2,1)} %convert_element_type.711), channel_id=1, source_target_pairs={{0,1},{1,0},{2,3},{3,2},{4,5},{5,4},{6,7},{7,6},{8,9},{9,8},{10,11... | collective-permute-start | bytes 1572872 | tf_op jit(solution)/shard_map/ppermute | solution.py:165
  139.5 16.8 %collective-permute-start.14 = (bf16[256,256]{1,0:T(8,128)(2,1)S(1)}, bf16[256,256]{1,0:T(8,128)(2,1)S(1)}, u32[]{:S(2)}, u32[]{:S(2)}) collective-permute-start(bf16[256,256]{1,0:T(8,128)(2,1)S(1)} %convolution_convert_fusion.2), channel_id=1, source_target_pairs={{0,1},{1,0},{2,3},{3,2},{4,5},{5,4},{6,7},{7,6},{8,9},{9,8},{10,11... | collective-permute-start | bytes 393224 | tf_op jit(solution)/shard_map/ppermute | solution.py:165
  154.1 11.9 %collective-permute-start.102 = (bf16[64,1024]{1,0:T(8,128)(2,1)}, bf16[64,1024]{1,0:T(8,128)(2,1)}, u32[]{:S(2)}, u32[]{:S(2)}) collective-permute-start(bf16[64,1024]{1,0:T(8,128)(2,1)} %dynamic-slice_convert_fusion.2), channel_id=1, source_target_pairs={{8,0},{16,8},{24,16},{28,24},{20,28},{12,20},{4,12},{0,4},{9,1},{1... | collective-permute-start | bytes 393224 | tf_op jit(solution)/shard_map/ppermute | solution.py:190
  156.3 16.4 %collective-permute-start.88 = (bf16[64,1024]{1,0:T(8,128)(2,1)}, bf16[64,1024]{1,0:T(8,128)(2,1)S(1)}, u32[]{:S(2)}, u32[]{:S(2)}) collective-permute-start(bf16[64,1024]{1,0:T(8,128)(2,1)} %dynamic-slice_convert_fusion.3), channel_id=1, source_target_pairs={{0,8},{8,16},{16,24},{24,28},{28,20},{20,12},{12,4},{4,0},{1,9},{9... | collective-permute-start | bytes 393224 | tf_op jit(solution)/shard_map/ppermute | solution.py:190
  172.6 50.6 %collective-permute-start.15 = (bf16[3,256,256]{2,1,0:T(8,128)(2,1)S(1)}, bf16[3,256,256]{2,1,0:T(8,128)(2,1)S(1)}, u32[]{:S(2)}, u32[]{:S(2)}) collective-permute-start(bf16[3,256,256]{2,1,0:T(8,128)(2,1)S(1)} %slice.200), channel_id=1, source_target_pairs={{0,1},{1,0},{2,3},{3,2},{4,5},{5,4},{6,7},{7,6},{8,9},{9,8},{10,11... | collective-permute-start | bytes 1179656 | tf_op jit(solution)/shard_map/ppermute | solution.py:165
  217.0 14.1 %collective-permute-start.105 = (bf16[64,1024]{1,0:T(8,128)(2,1)S(1)}, bf16[64,1024]{1,0:T(8,128)(2,1)S(1)}, u32[]{:S(2)}, u32[]{:S(2)}) collective-permute-start(bf16[64,1024]{1,0:T(8,128)(2,1)S(1)} %add_convert_fusion.20), channel_id=1, source_target_pairs={{8,0},{16,8},{24,16},{28,24},{20,28},{12,20},{4,12},{0,4},{9,1},{1... | collective-permute-start | bytes 393224 | tf_op jit(solution)/shard_map/ppermute | solution.py:190
  218.3 12.8 %collective-permute-start.91 = (bf16[64,1024]{1,0:T(8,128)(2,1)S(1)}, bf16[64,1024]{1,0:T(8,128)(2,1)S(1)}, u32[]{:S(2)}, u32[]{:S(2)}) collective-permute-start(bf16[64,1024]{1,0:T(8,128)(2,1)S(1)} %add_convert_fusion.27), channel_id=1, source_target_pairs={{0,8},{8,16},{16,24},{24,28},{28,20},{20,12},{12,4},{4,0},{1,9},{9... | collective-permute-start | bytes 393224 | tf_op jit(solution)/shard_map/ppermute | solution.py:190
  221.9 9.9 %collective-permute-start.137 = (bf16[64,1024]{1,0:T(8,128)(2,1)S(1)}, bf16[64,1024]{1,0:T(8,128)(2,1)S(1)}, u32[]{:S(2)}, u32[]{:S(2)}) collective-permute-start(bf16[64,1024]{1,0:T(8,128)(2,1)S(1)} %add_convert_fusion.6), channel_id=1, source_target_pairs={{8,0},{16,8},{24,16},{28,24},{20,28},{12,20},{4,12},{0,4},{9,1},{1... | collective-permute-start | bytes 393224 | tf_op jit(solution)/shard_map/ppermute | solution.py:190
  223.3 9.9 %collective-permute-start.123 = (bf16[64,1024]{1,0:T(8,128)(2,1)S(1)}, bf16[64,1024]{1,0:T(8,128)(2,1)S(1)}, u32[]{:S(2)}, u32[]{:S(2)}) collective-permute-start(bf16[64,1024]{1,0:T(8,128)(2,1)S(1)} %add_convert_fusion.13), channel_id=1, source_target_pairs={{0,8},{8,16},{16,24},{24,28},{28,20},{20,12},{12,4},{4,0},{1,9},{9... | collective-permute-start | bytes 393224 | tf_op jit(solution)/shard_map/ppermute | solution.py:190
  231.2 88.0 %collective-permute-start.57 = (bf16[256,1024]{1,0:T(8,128)(2,1)}, bf16[256,1024]{1,0:T(8,128)(2,1)}, u32[]{:S(2)}, u32[]{:S(2)}) collective-permute-start(bf16[256,1024]{1,0:T(8,128)(2,1)} %collective-permute-done.17), channel_id=1, source_target_pairs={{0,1},{1,0},{2,3},{3,2},{4,5},{5,4},{6,7},{7,6},{8,9},{9,8},{10,11... | collective-permute-start | bytes 1572872 | tf_op jit(solution)/shard_map/ppermute | solution.py:165
  231.8 15.4 %collective-permute-start.106 = (bf16[64,1024]{1,0:T(8,128)(2,1)S(1)}, bf16[64,1024]{1,0:T(8,128)(2,1)S(1)}, u32[]{:S(2)}, u32[]{:S(2)}) collective-permute-start(bf16[64,1024]{1,0:T(8,128)(2,1)S(1)} %add_convert_fusion.19), channel_id=1, source_target_pairs={{8,0},{16,8},{24,16},{28,24},{20,28},{12,20},{4,12},{0,4},{9,1},{1... | collective-permute-start | bytes 393224 | tf_op jit(solution)/shard_map/ppermute | solution.py:190
  233.2 15.4 %collective-permute-start.92 = (bf16[64,1024]{1,0:T(8,128)(2,1)S(1)}, bf16[64,1024]{1,0:T(8,128)(2,1)S(1)}, u32[]{:S(2)}, u32[]{:S(2)}) collective-permute-start(bf16[64,1024]{1,0:T(8,128)(2,1)S(1)} %add_convert_fusion.26), channel_id=1, source_target_pairs={{0,8},{8,16},{16,24},{24,28},{28,20},{20,12},{12,4},{4,0},{1,9},{9... | collective-permute-start | bytes 393224 | tf_op jit(solution)/shard_map/ppermute | solution.py:190
  234.0 18.6 %collective-permute-start.138 = (bf16[64,1024]{1,0:T(8,128)(2,1)S(1)}, bf16[64,1024]{1,0:T(8,128)(2,1)S(1)}, u32[]{:S(2)}, u32[]{:S(2)}) collective-permute-start(bf16[64,1024]{1,0:T(8,128)(2,1)S(1)} %add_convert_fusion.5), channel_id=1, source_target_pairs={{8,0},{16,8},{24,16},{28,24},{20,28},{12,20},{4,12},{0,4},{9,1},{1... | collective-permute-start | bytes 393224 | tf_op jit(solution)/shard_map/ppermute | solution.py:190
  247.2 10.9 %collective-permute-start.124 = (bf16[64,1024]{1,0:T(8,128)(2,1)S(1)}, bf16[64,1024]{1,0:T(8,128)(2,1)S(1)}, u32[]{:S(2)}, u32[]{:S(2)}) collective-permute-start(bf16[64,1024]{1,0:T(8,128)(2,1)S(1)} %add_convert_fusion.12), channel_id=1, source_target_pairs={{0,8},{8,16},{16,24},{24,28},{28,20},{20,12},{12,4},{4,0},{1,9},{9... | collective-permute-start | bytes 393224 | tf_op jit(solution)/shard_map/ppermute | solution.py:190
  252.5 70.3 %collective-permute-start.19 = (bf16[3,256,256]{2,1,0:T(8,128)(2,1)S(1)}, bf16[3,256,256]{2,1,0:T(8,128)(2,1)S(1)}, u32[]{:S(2)}, u32[]{:S(2)}) collective-permute-start(bf16[3,256,256]{2,1,0:T(8,128)(2,1)S(1)} %slice.210), channel_id=1, source_target_pairs={{0,1},{1,0},{2,3},{3,2},{4,5},{5,4},{6,7},{7,6},{8,9},{9,8},{10,11... | collective-permute-start | bytes 1179656 | tf_op jit(solution)/shard_map/ppermute | solution.py:165
  256.5 9.1 %collective-permute-start.21 = (bf16[192,256]{1,0:T(8,128)(2,1)}, bf16[192,256]{1,0:T(8,128)(2,1)}, u32[]{:S(2)}, u32[]{:S(2)}) collective-permute-start(bf16[192,256]{1,0:T(8,128)(2,1)} %get-tuple-element.74), channel_id=1, source_target_pairs={{0,8},{8,16},{16,24},{24,28},{28,20},{20,12},{12,4},{4,0},{1,9},{9... | collective-permute-start | bytes 294920 | tf_op jit(solution)/shard_map/ppermute | solution.py:190
  263.0 120.1 %collective-permute-start.35 = (bf16[192,256]{1,0:T(8,128)(2,1)}, bf16[192,256]{1,0:T(8,128)(2,1)}, u32[]{:S(2)}, u32[]{:S(2)}) collective-permute-start(bf16[192,256]{1,0:T(8,128)(2,1)} %get-tuple-element.75), channel_id=1, source_target_pairs={{8,0},{16,8},{24,16},{28,24},{20,28},{12,20},{4,12},{0,4},{9,1},{1... | collective-permute-start | bytes 294920 | tf_op jit(solution)/shard_map/ppermute | solution.py:190
  317.0 13.4 %collective-permute-start.109 = (bf16[64,1024]{1,0:T(8,128)(2,1)S(1)}, bf16[64,1024]{1,0:T(8,128)(2,1)S(1)}, u32[]{:S(2)}, u32[]{:S(2)}) collective-permute-start(bf16[64,1024]{1,0:T(8,128)(2,1)S(1)} %get-tuple-element.49), channel_id=1, source_target_pairs={{8,0},{16,8},{24,16},{28,24},{20,28},{12,20},{4,12},{0,4},{9,1},{1... | collective-permute-start | bytes 393224 | tf_op jit(solution)/shard_map/ppermute | solution.py:195
  318.1 13.8 %collective-permute-start.95 = (bf16[64,1024]{1,0:T(8,128)(2,1)S(1)}, bf16[64,1024]{1,0:T(8,128)(2,1)S(1)}, u32[]{:S(2)}, u32[]{:S(2)}) collective-permute-start(bf16[64,1024]{1,0:T(8,128)(2,1)S(1)} %get-tuple-element.47), channel_id=1, source_target_pairs={{0,8},{8,16},{16,24},{24,28},{28,20},{20,12},{12,4},{4,0},{1,9},{9... | collective-permute-start | bytes 393224 | tf_op jit(solution)/shard_map/ppermute | solution.py:195
  319.2 13.4 %collective-permute-start.141 = (bf16[64,1024]{1,0:T(8,128)(2,1)S(1)}, bf16[64,1024]{1,0:T(8,128)(2,1)S(1)}, u32[]{:S(2)}, u32[]{:S(2)}) collective-permute-start(bf16[64,1024]{1,0:T(8,128)(2,1)S(1)} %get-tuple-element.45), channel_id=1, source_target_pairs={{8,0},{16,8},{24,16},{28,24},{20,28},{12,20},{4,12},{0,4},{9,1},{1... | collective-permute-start | bytes 393224 | tf_op jit(solution)/shard_map/ppermute | solution.py:195
  332.6 134.7 %collective-permute-start.20 = (bf16[256,1024]{1,0:T(8,128)(2,1)S(1)}, bf16[256,1024]{1,0:T(8,128)(2,1)S(1)}, u32[]{:S(2)}, u32[]{:S(2)}) collective-permute-start(bf16[256,1024]{1,0:T(8,128)(2,1)S(1)} %fusion.55), channel_id=1, source_target_pairs={{0,2},{1,3},{2,0},{3,1},{4,6},{5,7},{6,4},{7,5},{8,10},{9,11},{10,... | collective-permute-start | bytes 1572872 | tf_op jit(solution)/shard_map/ppermute | solution.py:165
  335.0 19.7 %collective-permute-start.25 = (bf16[192,256]{1,0:T(8,128)(2,1)S(1)}, bf16[192,256]{1,0:T(8,128)(2,1)S(1)}, u32[]{:S(2)}, u32[]{:S(2)}) collective-permute-start(bf16[192,256]{1,0:T(8,128)(2,1)S(1)} %fusion.138), channel_id=1, source_target_pairs={{0,8},{8,16},{16,24},{24,28},{28,20},{20,12},{12,4},{4,0},{1,9},{9... | collective-permute-start | bytes 294920 | tf_op jit(solution)/shard_map/ppermute | solution.py:190
  335.3 27.6 %collective-permute-start.110 = (bf16[64,1024]{1,0:T(8,128)(2,1)S(1)}, bf16[64,1024]{1,0:T(8,128)(2,1)S(1)}, u32[]{:S(2)}, u32[]{:S(2)}) collective-permute-start(bf16[64,1024]{1,0:T(8,128)(2,1)S(1)} %collective-permute-done.109), channel_id=1, source_target_pairs={{8,0},{16,8},{24,16},{28,24},{20,28},{12,20},{4,12},{0,4},{9,1},{1... | collective-permute-start | bytes 393224 | tf_op jit(solution)/shard_map/ppermute | solution.py:195
  353.0 11.8 %collective-permute-start.96 = (bf16[64,1024]{1,0:T(8,128)(2,1)S(1)}, bf16[64,1024]{1,0:T(8,128)(2,1)S(1)}, u32[]{:S(2)}, u32[]{:S(2)}) collective-permute-start(bf16[64,1024]{1,0:T(8,128)(2,1)S(1)} %collective-permute-done.95), channel_id=1, source_target_pairs={{0,8},{8,16},{16,24},{24,28},{28,20},{20,12},{12,4},{4,0},{1,9},{9... | collective-permute-start | bytes 393224 | tf_op jit(solution)/shard_map/ppermute | solution.py:195
  364.8 19.4 %collective-permute-start.26 = (bf16[192,256]{1,0:T(8,128)(2,1)S(1)}, bf16[192,256]{1,0:T(8,128)(2,1)S(1)}, u32[]{:S(2)}, u32[]{:S(2)}) collective-permute-start(bf16[192,256]{1,0:T(8,128)(2,1)S(1)} %fusion.141), channel_id=1, source_target_pairs={{0,8},{8,16},{16,24},{24,28},{28,20},{20,12},{12,4},{4,0},{1,9},{9... | collective-permute-start | bytes 294920 | tf_op jit(solution)/shard_map/ppermute | solution.py:190
  371.9 29.8 %collective-permute-start.111 = (bf16[64,1024]{1,0:T(8,128)(2,1)S(1)}, bf16[64,1024]{1,0:T(8,128)(2,1)S(1)}, u32[]{:S(2)}, u32[]{:S(2)}) collective-permute-start(bf16[64,1024]{1,0:T(8,128)(2,1)S(1)} %collective-permute-done.110), channel_id=1, source_target_pairs={{8,0},{16,8},{24,16},{28,24},{20,28},{12,20},{4,12},{0,4},{9,1},{1... | collective-permute-start | bytes 393224 | tf_op jit(solution)/shard_map/ppermute | solution.py:195
  382.0 20.6 %collective-permute-start.97 = (bf16[64,1024]{1,0:T(8,128)(2,1)S(1)}, bf16[64,1024]{1,0:T(8,128)(2,1)S(1)}, u32[]{:S(2)}, u32[]{:S(2)}) collective-permute-start(bf16[64,1024]{1,0:T(8,128)(2,1)S(1)} %collective-permute-done.96), channel_id=1, source_target_pairs={{0,8},{8,16},{16,24},{24,28},{28,20},{20,12},{12,4},{4,0},{1,9},{9... | collective-permute-start | bytes 393224 | tf_op jit(solution)/shard_map/ppermute | solution.py:195
  383.1 20.8 %collective-permute-start.143 = (bf16[64,1024]{1,0:T(8,128)(2,1)S(1)}, bf16[64,1024]{1,0:T(8,128)(2,1)S(1)}, u32[]{:S(2)}, u32[]{:S(2)}) collective-permute-start(bf16[64,1024]{1,0:T(8,128)(2,1)S(1)} %collective-permute-done.142), channel_id=1, source_target_pairs={{8,0},{16,8},{24,16},{28,24},{20,28},{12,20},{4,12},{0,4},{9,1},{1... | collective-permute-start | bytes 393224 | tf_op jit(solution)/shard_map/ppermute | solution.py:195
  401.7 9.0 %collective-permute-start.27 = (bf16[192,256]{1,0:T(8,128)(2,1)S(1)}, bf16[192,256]{1,0:T(8,128)(2,1)S(1)}, u32[]{:S(2)}, u32[]{:S(2)}) collective-permute-start(bf16[192,256]{1,0:T(8,128)(2,1)S(1)} %get-tuple-element.72), channel_id=1, source_target_pairs={{0,8},{8,16},{16,24},{24,28},{28,20},{20,12},{12,4},{4,0},{1,9},{9... | collective-permute-start | bytes 294920 | tf_op jit(solution)/shard_map/ppermute | solution.py:190
  402.6 8.8 %collective-permute-start.36 = (bf16[192,256]{1,0:T(8,128)(2,1)S(1)}, bf16[192,256]{1,0:T(8,128)(2,1)S(1)}, u32[]{:S(2)}, u32[]{:S(2)}) collective-permute-start(bf16[192,256]{1,0:T(8,128)(2,1)S(1)} %get-tuple-element.73), channel_id=1, source_target_pairs={{8,0},{16,8},{24,16},{28,24},{20,28},{12,20},{4,12},{0,4},{9,1},{1... | collective-permute-start | bytes 294920 | tf_op jit(solution)/shard_map/ppermute | solution.py:190
  407.8 39.2 %collective-permute-start.112 = (bf16[64,1024]{1,0:T(8,128)(2,1)S(1)}, bf16[64,1024]{1,0:T(8,128)(2,1)S(1)}, u32[]{:S(2)}, u32[]{:S(2)}) collective-permute-start(bf16[64,1024]{1,0:T(8,128)(2,1)S(1)} %collective-permute-done.111), channel_id=1, source_target_pairs={{8,0},{16,8},{24,16},{28,24},{20,28},{12,20},{4,12},{0,4},{9,1},{1... | collective-permute-start | bytes 393224 | tf_op jit(solution)/shard_map/ppermute | solution.py:195
  409.4 38.9 %collective-permute-start.98 = (bf16[64,1024]{1,0:T(8,128)(2,1)S(1)}, bf16[64,1024]{1,0:T(8,128)(2,1)S(1)}, u32[]{:S(2)}, u32[]{:S(2)}) collective-permute-start(bf16[64,1024]{1,0:T(8,128)(2,1)S(1)} %collective-permute-done.97), channel_id=1, source_target_pairs={{0,8},{8,16},{16,24},{24,28},{28,20},{20,12},{12,4},{4,0},{1,9},{9... | collective-permute-start | bytes 393224 | tf_op jit(solution)/shard_map/ppermute | solution.py:195
  410.6 38.6 %collective-permute-start.144 = (bf16[64,1024]{1,0:T(8,128)(2,1)S(1)}, bf16[64,1024]{1,0:T(8,128)(2,1)S(1)}, u32[]{:S(2)}, u32[]{:S(2)}) collective-permute-start(bf16[64,1024]{1,0:T(8,128)(2,1)S(1)} %collective-permute-done.143), channel_id=1, source_target_pairs={{8,0},{16,8},{24,16},{28,24},{20,28},{12,20},{4,12},{0,4},{9,1},{1... | collective-permute-start | bytes 393224 | tf_op jit(solution)/shard_map/ppermute | solution.py:195
  449.3 15.8 %collective-permute-start.38 = (bf16[192,256]{1,0:T(8,128)(2,1)S(1)}, bf16[192,256]{1,0:T(8,128)(2,1)S(1)}, u32[]{:S(2)}, u32[]{:S(2)}) collective-permute-start(bf16[192,256]{1,0:T(8,128)(2,1)S(1)} %fusion.158), channel_id=1, source_target_pairs={{8,0},{16,8},{24,16},{28,24},{20,28},{12,20},{4,12},{0,4},{9,1},{1... | collective-permute-start | bytes 294920 | tf_op jit(solution)/shard_map/ppermute | solution.py:190
  452.1 14.4 %collective-permute-start.29 = (bf16[192,256]{1,0:T(8,128)(2,1)S(1)}, bf16[192,256]{1,0:T(8,128)(2,1)S(1)}, u32[]{:S(2)}, u32[]{:S(2)}) collective-permute-start(bf16[192,256]{1,0:T(8,128)(2,1)S(1)} %collective-permute-done.28), channel_id=1, source_target_pairs={{0,8},{8,16},{16,24},{24,28},{28,20},{20,12},{12,4},{4,0},{1,9},{9... | collective-permute-start | bytes 294920 | tf_op jit(solution)/shard_map/ppermute | solution.py:195
  453.0 17.3 %collective-permute-start.113 = (bf16[64,1024]{1,0:T(8,128)(2,1)S(1)}, bf16[64,1024]{1,0:T(8,128)(2,1)S(1)}, u32[]{:S(2)}, u32[]{:S(2)}) collective-permute-start(bf16[64,1024]{1,0:T(8,128)(2,1)S(1)} %collective-permute-done.112), channel_id=1, source_target_pairs={{8,0},{16,8},{24,16},{28,24},{20,28},{12,20},{4,12},{0,4},{9,1},{1... | collective-permute-start | bytes 393224 | tf_op jit(solution)/shard_map/ppermute | solution.py:195
  463.4 7.5 %collective-permute-start.99 = (bf16[64,1024]{1,0:T(8,128)(2,1)S(1)}, bf16[64,1024]{1,0:T(8,128)(2,1)S(1)}, u32[]{:S(2)}, u32[]{:S(2)}) collective-permute-start(bf16[64,1024]{1,0:T(8,128)(2,1)S(1)} %collective-permute-done.98), channel_id=1, source_target_pairs={{0,8},{8,16},{16,24},{24,28},{28,20},{20,12},{12,4},{4,0},{1,9},{9... | collective-permute-start | bytes 393224 | tf_op jit(solution)/shard_map/ppermute | solution.py:195
  465.0 7.4 %collective-permute-start.145 = (bf16[64,1024]{1,0:T(8,128)(2,1)S(1)}, bf16[64,1024]{1,0:T(8,128)(2,1)S(1)}, u32[]{:S(2)}, u32[]{:S(2)}) collective-permute-start(bf16[64,1024]{1,0:T(8,128)(2,1)S(1)} %collective-permute-done.144), channel_id=1, source_target_pairs={{8,0},{16,8},{24,16},{28,24},{20,28},{12,20},{4,12},{0,4},{9,1},{1... | collective-permute-start | bytes 393224 | tf_op jit(solution)/shard_map/ppermute | solution.py:195
  467.2 7.4 %collective-permute-start.39 = (bf16[192,256]{1,0:T(8,128)(2,1)S(1)}, bf16[192,256]{1,0:T(8,128)(2,1)S(1)}, u32[]{:S(2)}, u32[]{:S(2)}) collective-permute-start(bf16[192,256]{1,0:T(8,128)(2,1)S(1)} %fusion.161), channel_id=1, source_target_pairs={{8,0},{16,8},{24,16},{28,24},{20,28},{12,20},{4,12},{0,4},{9,1},{1... | collective-permute-start | bytes 294920 | tf_op jit(solution)/shard_map/ppermute | solution.py:190
  477.6 15.2 %collective-permute-start.115 = (bf16[64,1024]{1,0:T(8,128)(2,1)S(1)}, bf16[64,1024]{1,0:T(8,128)(2,1)S(1)}, u32[]{:S(2)}, u32[]{:S(2)}) collective-permute-start(bf16[64,1024]{1,0:T(8,128)(2,1)S(1)} %collective-permute-done.114), channel_id=1, source_target_pairs={{8,0},{16,8},{24,16},{28,24},{20,28},{12,20},{4,12},{0,4},{9,1},{1... | collective-permute-start | bytes 393224 | tf_op jit(solution)/shard_map/ppermute | solution.py:195
  479.1 14.3 %collective-permute-start.101 = (bf16[64,1024]{1,0:T(8,128)(2,1)S(1)}, bf16[64,1024]{1,0:T(8,128)(2,1)S(1)}, u32[]{:S(2)}, u32[]{:S(2)}) collective-permute-start(bf16[64,1024]{1,0:T(8,128)(2,1)S(1)} %collective-permute-done.100), channel_id=1, source_target_pairs={{0,8},{8,16},{16,24},{24,28},{28,20},{20,12},{12,4},{4,0},{1,9},{9... | collective-permute-start | bytes 393224 | tf_op jit(solution)/shard_map/ppermute | solution.py:195
  479.8 13.7 %collective-permute-start.147 = (bf16[64,1024]{1,0:T(8,128)(2,1)S(1)}, bf16[64,1024]{1,0:T(8,128)(2,1)S(1)}, u32[]{:S(2)}, u32[]{:S(2)}) collective-permute-start(bf16[64,1024]{1,0:T(8,128)(2,1)S(1)} %collective-permute-done.146), channel_id=1, source_target_pairs={{8,0},{16,8},{24,16},{28,24},{20,28},{12,20},{4,12},{0,4},{9,1},{1... | collective-permute-start | bytes 393224 | tf_op jit(solution)/shard_map/ppermute | solution.py:195
  481.3 14.8 %collective-permute-start.133 = (bf16[64,1024]{1,0:T(8,128)(2,1)S(1)}, bf16[64,1024]{1,0:T(8,128)(2,1)S(1)}, u32[]{:S(2)}, u32[]{:S(2)}) collective-permute-start(bf16[64,1024]{1,0:T(8,128)(2,1)S(1)} %collective-permute-done.132), channel_id=1, source_target_pairs={{0,8},{8,16},{16,24},{24,28},{28,20},{20,12},{12,4},{4,0},{1,9},{9... | collective-permute-start | bytes 393224 | tf_op jit(solution)/shard_map/ppermute | solution.py:195
  491.3 7.3 %collective-permute-start.42 = (bf16[192,256]{1,0:T(8,128)(2,1)S(1)}, bf16[192,256]{1,0:T(8,128)(2,1)S(1)}, u32[]{:S(2)}, u32[]{:S(2)}) collective-permute-start(bf16[192,256]{1,0:T(8,128)(2,1)S(1)} %get-tuple-element.61), channel_id=1, source_target_pairs={{8,0},{16,8},{24,16},{28,24},{20,28},{12,20},{4,12},{0,4},{9,1},{1... | collective-permute-start | bytes 294920 | tf_op jit(solution)/shard_map/ppermute | solution.py:195
  492.8 7.3 %collective-permute-start.33 = (bf16[192,256]{1,0:T(8,128)(2,1)S(1)}, bf16[192,256]{1,0:T(8,128)(2,1)S(1)}, u32[]{:S(2)}, u32[]{:S(2)}) collective-permute-start(bf16[192,256]{1,0:T(8,128)(2,1)S(1)} %collective-permute-done.32), channel_id=1, source_target_pairs={{0,8},{8,16},{16,24},{24,28},{28,20},{20,12},{12,4},{4,0},{1,9},{9... | collective-permute-start | bytes 294920 | tf_op jit(solution)/shard_map/ppermute | solution.py:195
  (163 other events, 1057.2 us)
